TPU v7x, 256 devices: a whole 4x4x8 slice. The times are simulated.
256 devices in a mesh: db: 16 (over y_lo, x, core), pb: 16 (over z, y_hi).
Axes of the slice: x: 4, y: 4 (y_hi: 2, y_lo: 2; y = y_hi * 2 + y_lo), z: 8, core: 2. Of those that a mesh axis runs over, the one named last changes fastest.
Arguments:
- queries: bfloat16 [512, 512, 1280], P(('db', 'pb')), may hold values from -4 to 4
- query_scale: bfloat16 [512, 512], P(('db', 'pb')), may hold values from 0.0099487305 to 0.049804688
- query_mask: int32 [512, 512], P(('db', 'pb')), may hold values 0 or 1
- query_len: int32 [512], P(('db', 'pb')), may hold values from 64 to 512
- targets: bfloat16 [2048, 128, 1280], P(('db', 'pb')), may hold values from -4 to 4
- target_scale: bfloat16 [2048, 128], P(('db', 'pb')), may hold values from 0.0099487305 to 0.049804688
- target_mask: int32 [2048, 128], P(('db', 'pb')), may hold values 0 or 1
- target_len: int32 [2048], P(('db', 'pb')), may hold values from 32 to 128
- hit_ids: int32 [512, 8], P(('db', 'pb')), may hold values from 0 to 2047, as said below
Outputs:
- band: float32 [2, 2048, 2, 640], P(None, ('db', 'pb'))
- rescore: float32 [512, 8], P(('db', 'pb'))
Inputs may be any that keep to these rules, and one draw needn't show every extreme that they name: `hit_ids`: the hits of the query tiles of shard a * 16 + b name target blocks of shards a * 16 + e, e < 16. Over the hits of one shard's query tiles, at most 2 name target blocks of one such shard, and in every shard's list some shard is named exactly 2 times; hits may repeat.
All inputs are finite; a program needn't handle non-finite values. No bound on the sum of `query_mask` or of `target_mask` on one device may be relied on, other than what follows from the above.
Results may differ from a plain program's by a relative error of at most 0.00045.
Values may be sent and summed in bfloat16 or wider, within the bound.
A program may use at most 128 MiB of HBM per device.

v0:
```python
import jax
import jax.numpy as jnp
from jax import lax
from jax.sharding import PartitionSpec as P


def passed_along(value, axis, by):
    peers = lax.axis_size(axis)
    return lax.ppermute(value, axis, [(i, (i + by) % peers) for i in range(peers)])


def weights_of(scale, mask, length):
    position = jnp.arange(scale.shape[1], dtype=jnp.int32)
    live = (mask == 1) & (position[None, :] < length[:, None])
    return jnp.where(live, scale, jnp.zeros_like(scale))


def diagonal_table(target_rows):
    row_index = jnp.arange(target_rows, dtype=jnp.int32)
    offset = jnp.arange(2 * target_rows, dtype=jnp.int32)
    wanted = row_index[:, None, None] - row_index[None, :, None] + target_rows - 1
    table = (wanted == offset[None, None, :]).astype(jnp.float32)
    return table.reshape(target_rows * target_rows, 2 * target_rows)


def diagonal_band(scores):
    leading = scores.shape[:-2]
    query_rows = scores.shape[-2]
    target_rows = scores.shape[-1]
    blocks = query_rows // target_rows
    flat = scores.reshape(leading + (blocks, target_rows * target_rows))
    parts = jnp.dot(
        flat,
        diagonal_table(target_rows),
        precision=lax.Precision.HIGHEST,
        preferred_element_type=jnp.float32,
    )
    lower = parts[..., :target_rows]
    upper = parts[..., target_rows:]
    zero_row = jnp.zeros(leading + (1, target_rows), jnp.float32)
    folded = jnp.concatenate([lower, zero_row], axis=-2) + jnp.concatenate(
        [zero_row, upper], axis=-2
    )
    diagonals = folded.reshape(leading + ((blocks + 1) * target_rows,))
    shifted = jnp.concatenate(
        [jnp.zeros(leading + (1,), jnp.float32), diagonals[..., :-1]], axis=-1
    )
    return diagonals + shifted


def cross_band(query_tiles, query_w, target_rows, target_w):
    target_count = target_rows.shape[0]
    group_size = 4
    grouped = target_rows.reshape((target_count // group_size, group_size) + target_rows.shape[1:])
    grouped_w = target_w.reshape(target_count // group_size, group_size, target_w.shape[1])
    query_wf = query_w.astype(jnp.float32)

    def one_group(operands):
        rows, rows_w = operands
        raw = jnp.einsum("kid,tjd->tkij", query_tiles, rows, preferred_element_type=jnp.float32)
        scaled = raw * query_wf[None, :, :, None] * rows_w.astype(jnp.float32)[:, None, None, :]
        return diagonal_band(scaled)

    result = lax.map(one_group, (grouped, grouped_w))
    return result.reshape((target_count,) + result.shape[2:])


def fetch_hits(hit_ids, targets, target_weight):
    query_count = hit_ids.shape[0]
    hit_count = hit_ids.shape[1]
    target_count = targets.shape[0]
    groups = lax.axis_size("pb")
    capacity = (query_count * hit_count + groups - 1) // groups + 1
    flat_ids = hit_ids.reshape(-1)
    owners = flat_ids // target_count % groups
    local_ids = flat_ids % target_count
    ordinal = jnp.arange(flat_ids.shape[0], dtype=jnp.int32)
    before = (owners[:, None] == owners[None, :]) & (ordinal[:, None] > ordinal[None, :])
    ranks = jnp.sum(before.astype(jnp.int32), axis=1)
    slots = owners * capacity + ranks
    onehot = (slots[:, None] == jnp.arange(groups * capacity, dtype=jnp.int32)[None, :]).astype(
        jnp.int32
    )
    requests = jnp.sum(onehot * local_ids[:, None], axis=0).reshape(groups, capacity)
    wanted = lax.all_to_all(requests, "pb", split_axis=0, concat_axis=0, tiled=True)
    rows = jnp.take(targets, wanted, axis=0)
    rows_w = jnp.take(target_weight, wanted, axis=0)
    fetched = lax.all_to_all(rows, "pb", split_axis=0, concat_axis=0, tiled=True)
    fetched_w = lax.all_to_all(rows_w, "pb", split_axis=0, concat_axis=0, tiled=True)
    return (fetched, fetched_w, slots)


def rescore_hits(queries, query_weight, fetched, fetched_w, slots, hit_count):
    query_count = queries.shape[0]
    groups_slots = fetched.shape[0] * fetched.shape[1]
    target_rows = fetched.shape[2]
    chosen = fetched.reshape((groups_slots,) + fetched.shape[2:])[slots]
    chosen = chosen.reshape((query_count, hit_count) + fetched.shape[2:])
    chosen_w = fetched_w.reshape(groups_slots, target_rows)[slots].reshape(
        query_count, hit_count, target_rows
    )
    raw = jnp.einsum("kid,khjd->khij", queries, chosen, preferred_element_type=jnp.float32)
    scaled = (
        raw
        * query_weight.astype(jnp.float32)[:, None, :, None]
        * chosen_w.astype(jnp.float32)[:, :, None, :]
    )
    banded = diagonal_band(scaled)
    return jnp.sum(jnp.maximum(banded, 0.0), axis=-1) / banded.shape[-1]


def shards(
    queries,
    query_scale,
    query_mask,
    query_len,
    targets,
    target_scale,
    target_mask,
    target_len,
    hit_ids,
):
    query_weight = weights_of(query_scale, query_mask, query_len)
    target_weight = weights_of(target_scale, target_mask, target_len)
    pieces = []
    travelling = (queries, query_weight)
    for stop_index in range(2):
        travelling = passed_along((travelling[0], travelling[1]), "db", 1)
        pieces.append(cross_band(travelling[0], travelling[1], targets, target_weight))
    band = jnp.stack(pieces)
    fetched, fetched_w, slots = fetch_hits(hit_ids, targets, target_weight)
    rescore = rescore_hits(queries, query_weight, fetched, fetched_w, slots, hit_ids.shape[1])
    return (band, rescore)


def solution(mesh):
    in_specs = (
        P(("db", "pb"), None, None),
        P(("db", "pb"), None),
        P(("db", "pb"), None),
        P(("db", "pb")),
        P(("db", "pb"), None, None),
        P(("db", "pb"), None),
        P(("db", "pb"), None),
        P(("db", "pb")),
        P(("db", "pb"), None),
    )
    out_specs = (P(None, ("db", "pb"), None, None), P(("db", "pb"), None))
    return jax.shard_map(shards, mesh=mesh, in_specs=in_specs, out_specs=out_specs, check_vma=False)
```

profile of v0, /device:TPU:6, one launch (start us, length us, event | category | flops | bytes accessed | tf_op | source)
XLA Modules:
  0.0 327.4 jit_solution(17127702469199333368)
XLA Ops:
  0.6 0.8 reshape.445
  1.4 0.2 convert_reduce_fusion
  1.7 0.7 all_to_all.16
  2.4 11.2 %all-to-all-start = ((s32[16,1,2]{2,1,0:T(1,128)}), s32[16,1,2]{2,1,0:T(1,128)S(1)}, u32[]{:S(2)}, u32[]{:S(2)}) async-start(s32[16,1,2]{2,1,0:T(1,128)} %bitcast.24), calls=%async_computation | async-start | bytes 16384 | tf_op jit(solution)/shard_map/all_to_all | solution.py:85
  13.6 0.8 fusion.32
  14.4 9.2 %all-to-all-done = s32[16,1,2]{2,1,0:T(1,128)S(1)} async-done(((s32[16,1,2]{2,1,0:T(1,128)}), s32[16,1,2]{2,1,0:T(1,128)S(1)}, u32[]{:S(2)}, u32[]{:S(2)}) %all-to-all-start) | async-done | bytes 160 | tf_op jit(solution)/shard_map/all_to_all | solution.py:85
  23.8 0.1 copy.47
  23.9 0.6 gather_fusion.2
  24.5 0.7 broadcast_select_fusion.1
  25.2 3.5 %all-to-all-start.2 = ((bf16[16,2,128]{2,1,0:T(2,128)(2,1)}), bf16[16,2,128]{2,1,0:T(2,128)(2,1)S(1)}, u32[]{:S(2)}, u32[]{:S(2)}) async-start(bf16[16,2,128]{2,1,0:T(2,128)(2,1)} %broadcast_select_fusion.1), calls=%async_computation.2 | async-start | bytes 16384 | tf_op jit(solution)/shard_map/all_to_all | solution.py:89
  28.7 7.5 %gather_fusion = bf16[32,128,1280]{2,1,0:T(8,128)(2,1)} fusion(bf16[8,128,1280]{2,1,0:T(8,128)(2,1)} %param.17, s32[1024]{0:T(1024)S(1)} %pad_clamp_fusion.1), kind=kCustom, calls=%fused_computation | custom fusion | bytes 20971648 | tf_op jit(solution)/shard_map/jit(_take)/gather | solution.py:86
  36.2 10.2 %broadcast_select_fusion = bf16[16,2,128,1280]{3,2,1,0:T(8,128)(2,1)} fusion(bf16[16,2,128,1280]{3,2,1,0:T(8,128)(2,1)} %bitcast.140, pred[16,2]{1,0:T(8,128)(4,1)S(1)} %copy.47), kind=kLoop, calls=%fused_computation.35 | loop fusion | flops 5242880 | bytes 20971552 | tf_op jit(solution)/shard_map/jit(_take)/select_n | solution.py:86
  46.4 9.8 %all-to-all-start.1 = ((bf16[16,2,128,1280]{3,2,1,0:T(8,128)(2,1)}), bf16[16,2,128,1280]{3,2,1,0:T(8,128)(2,1)}, u32[]{:S(2)}, u32[]{:S(2)}) async-start(bf16[16,2,128,1280]{3,2,1,0:T(8,128)(2,1)} %broadcast_select_fusion), calls=%async_computation.1 | async-start | bytes 20971520 | tf_op jit(solution)/shard_map/all_to_all | solution.py:88
  56.4 0.7 collective-permute-start.1
  57.2 30.4 %collective-permute-done.1 = bf16[2,512]{1,0:T(2,128)(2,1)S(1)} collective-permute-done((bf16[2,512]{1,0:T(2,128)(2,1)S(1)}, bf16[2,512]{1,0:T(2,128)(2,1)S(1)}, u32[]{:S(2)}, u32[]{:S(2)}) %collective-permute-start.1) | collective-permute-done | bytes 2080 | tf_op jit(solution)/shard_map/ppermute | solution.py:9
  87.7 3.0 collective-permute-done.3
  90.6 0.6 gather_fusion.3
  91.2 0.9 collective-permute-start.2
  92.2 33.5 %while.28 = (s32[]{:T(128)}, f32[2,4,2,640]{3,2,1,0:T(2,128)S(1)}, bf16[2,4,128,1280]{3,2,1,0:T(8,128)(2,1)}, bf16[2,512,1280]{2,1,0:T(8,128)(2,1)}, f32[2,512]{...) while((s32[]{:T(128)}, f32[2,4,2,640]{3,2,1,0:T(2,128)S(1)}, ...), condition=%wide.region_1.2_spmd, body=%wide.region_0.1_spmd.sunk | while | flops 2958076416 | bytes 16909908 | solution.py:64
  92.2 5.0 %multiply_bitcast_fusion.5 = f32[4,2,512,128]{2,3,1,0:T(8,128)} fusion(bf16[2,512,1280]{2,1,0:T(8,128)(2,1)} %get-tuple-element.402, bf16[2,4,128,1280]{3,2,1,0:T(8,128)(2,1)} %get-tuple-element.401, s32[]{:T(128)} %get-tuple-element.392, f32[4,128]{1,0:T(4,128)S(1)} %bitcast_convert_fusion.5, f32[2,512]{1,0:T(2,128)S(1)} %get-tuple-element.403), kind=kOutput, calls=%fused_computation.10.clone.1 | convolution fusion | flops 1343225856 | bytes 6035968 | tf_op jit(solution)/shard_map/while/body/eval_jaxpr/kid,tjd->tkij/dot_general | solution.py:60
  97.2 1.9 copy.60
  99.1 1.9 reshape.501
  101.1 7.7 %fusion.62 = f32[4,2,4,256]{3,2,1,0:T(4,128)S(1)} fusion(f32[4,2,4,16384]{3,2,1,0:T(4,128)} %reshape.501, s32[16384]{0:T(1024)S(1)} %add_bitcast_fusion.5), kind=kOutput, calls=%fused_computation.6.clone.1 | convolution fusion | flops 1614807040 | bytes 2195456 | tf_op jit(solution)/shard_map/while/body/eval_jaxpr/dot_general | solution.py:32
  108.9 5.0 %multiply_bitcast_fusion.5 = f32[4,2,512,128]{2,3,1,0:T(8,128)} fusion(bf16[2,512,1280]{2,1,0:T(8,128)(2,1)} %get-tuple-element.402, bf16[2,4,128,1280]{3,2,1,0:T(8,128)(2,1)} %get-tuple-element.401, s32[]{:T(128)} %get-tuple-element.392, f32[4,128]{1,0:T(4,128)S(1)} %bitcast_convert_fusion.5, f32[2,512]{1,0:T(2,128)S(1)} %get-tuple-element.403), kind=kOutput, calls=%fused_computation.10.clone.1 | convolution fusion | flops 1343225856 | bytes 6035968 | tf_op jit(solution)/shard_map/while/body/eval_jaxpr/kid,tjd->tkij/dot_general | solution.py:60
  114.0 1.9 copy.60
  115.9 1.9 reshape.501
  117.8 7.7 %fusion.62 = f32[4,2,4,256]{3,2,1,0:T(4,128)S(1)} fusion(f32[4,2,4,16384]{3,2,1,0:T(4,128)} %reshape.501, s32[16384]{0:T(1024)S(1)} %add_bitcast_fusion.5), kind=kOutput, calls=%fused_computation.6.clone.1 | convolution fusion | flops 1614807040 | bytes 2195456 | tf_op jit(solution)/shard_map/while/body/eval_jaxpr/dot_general | solution.py:32
  125.5 0.1 bitcast_dynamic-update-slice_fusion.4
  125.7 34.0 %while.29 = (s32[]{:T(128)}, f32[2,4,2,640]{3,2,1,0:T(2,128)S(1)}, bf16[2,4,128,1280]{3,2,1,0:T(8,128)(2,1)}, bf16[2,512,1280]{2,1,0:T(8,128)(2,1)}, f32[2,512]{...) while((s32[]{:T(128)}, f32[2,4,2,640]{3,2,1,0:T(2,128)S(1)}, ...), condition=%wide.region_3.4_spmd, body=%wide.region_2.3_spmd.sunk | while | flops 2958076416 | bytes 16909908 | solution.py:64
  125.9 5.1 %multiply_bitcast_fusion.6 = f32[4,2,512,128]{2,3,1,0:T(8,128)} fusion(bf16[2,512,1280]{2,1,0:T(8,128)(2,1)} %get-tuple-element.381, bf16[2,4,128,1280]{3,2,1,0:T(8,128)(2,1)} %get-tuple-element.380, s32[]{:T(128)} %get-tuple-element.371, f32[4,128]{1,0:T(4,128)S(1)} %bitcast_convert_fusion.6, f32[2,512]{1,0:T(2,128)S(1)} %get-tuple-element.382), kind=kOutput, calls=%fused_computation.24.clone.1 | convolution fusion | flops 1343225856 | bytes 6035968 | tf_op jit(solution)/shard_map/while/body/eval_jaxpr/kid,tjd->tkij/dot_general | solution.py:60
  131.0 1.9 copy.61
  133.0 2.0 reshape.503
  134.9 7.7 %fusion.68 = f32[4,2,4,256]{3,2,1,0:T(4,128)S(1)} fusion(f32[4,2,4,16384]{3,2,1,0:T(4,128)} %reshape.503, s32[16384]{0:T(1024)S(1)} %add_bitcast_fusion.6), kind=kOutput, calls=%fused_computation.20.clone.1 | convolution fusion | flops 1614807040 | bytes 2195456 | tf_op jit(solution)/shard_map/while/body/eval_jaxpr/dot_general | solution.py:32
  142.7 0.1 bitcast_dynamic-update-slice_fusion.5
  142.8 5.1 %multiply_bitcast_fusion.6 = f32[4,2,512,128]{2,3,1,0:T(8,128)} fusion(bf16[2,512,1280]{2,1,0:T(8,128)(2,1)} %get-tuple-element.381, bf16[2,4,128,1280]{3,2,1,0:T(8,128)(2,1)} %get-tuple-element.380, s32[]{:T(128)} %get-tuple-element.371, f32[4,128]{1,0:T(4,128)S(1)} %bitcast_convert_fusion.6, f32[2,512]{1,0:T(2,128)S(1)} %get-tuple-element.382), kind=kOutput, calls=%fused_computation.24.clone.1 | convolution fusion | flops 1343225856 | bytes 6035968 | tf_op jit(solution)/shard_map/while/body/eval_jaxpr/kid,tjd->tkij/dot_general | solution.py:60
  147.9 1.9 copy.61
  149.8 2.0 reshape.503
  151.8 7.7 %fusion.68 = f32[4,2,4,256]{3,2,1,0:T(4,128)S(1)} fusion(f32[4,2,4,16384]{3,2,1,0:T(4,128)} %reshape.503, s32[16384]{0:T(1024)S(1)} %add_bitcast_fusion.6), kind=kOutput, calls=%fused_computation.20.clone.1 | convolution fusion | flops 1614807040 | bytes 2195456 | tf_op jit(solution)/shard_map/while/body/eval_jaxpr/dot_general | solution.py:32
  159.6 0.1 bitcast_dynamic-update-slice_fusion.5
  159.7 0.7 pad_maximum_fusion
  160.3 130.6 %all-to-all-done.1 = bf16[16,2,128,1280]{3,2,1,0:T(8,128)(2,1)} async-done(((bf16[16,2,128,1280]{3,2,1,0:T(8,128)(2,1)}), bf16[16,2,128,1280]{3,2,1,0:T(8,128)(2,1)}, u32[]{:S(2)}, u32[]{:S(2)}) %all-to-all-start.1) | async-done | bytes 10485792 | tf_op jit(solution)/shard_map/all_to_all | solution.py:88
  290.9 7.2 %gather_fusion.1 = bf16[16,128,1280]{2,1,0:T(8,128)(2,1)} fusion(bf16[32,128,1280]{2,1,0:T(8,128)(2,1)} %bitcast.28, s32[1024]{0:T(1024)S(1)} %pad_clamp_fusion), kind=kCustom, calls=%fused_computation.1 | custom fusion | bytes 10485824 | tf_op jit(solution)/shard_map/gather | solution.py:97
  298.2 8.2 %multiply_bitcast_fusion.2 = f32[2,8,512,128]{2,3,1,0:T(8,128)} fusion(bf16[2,8,128,1280]{3,2,1,0:T(8,128)(2,1)} %bitcast.142, bf16[2,512,1280]{2,1,0:T(8,128)(2,1)} %param.13, f32[2,8,128]{2,1,0:T(8,128)S(1)} %bitcast_convert_fusion.2, f32[2,512]{1,0:T(2,128)S(1)} %get-tuple-element.272), kind=kOutput, calls=%fused_computation.37 | convolution fusion | flops 2686451712 | bytes 12070912 | tf_op jit(solution)/shard_map/kid,khjd->khij/dot_general | solution.py:102
  306.3 5.4 %copy.51 = f32[2,8,512,128]{3,2,1,0:T(8,128)} copy(f32[2,8,512,128]{2,3,1,0:T(8,128)} %multiply_bitcast_fusion.2) | data formatting | bytes 8388608 | tf_op jit(solution)/shard_map/mul | solution.py:104
  311.7 5.6 %reshape.450 = f32[2,8,4,16384]{3,2,1,0:T(4,128)} reshape(f32[2,8,512,128]{3,2,1,0:T(8,128)} %copy.51) | data formatting | bytes 8388608 | tf_op jit(solution)/shard_map/reshape | solution.py:31
  317.3 9.3 %fusion.23 = f32[2,8,4,256]{3,2,1,0:T(4,128)S(1)} fusion(f32[2,8,4,16384]{3,2,1,0:T(4,128)} %reshape.450, s32[16384]{0:T(1024)S(1)} %add_bitcast_fusion.2), kind=kOutput, calls=%fused_computation.34 | convolution fusion | flops 3225419776 | bytes 4325376 | tf_op jit(solution)/shard_map/dot_general | solution.py:32
  326.7 0.2 maximum_reduce_fusion
  326.8 0.6 broadcast_multiply_fusion
  (56 shorter events, 1.1 us)
Async XLA Ops:
  2.4 21.1 %all-to-all-start = ((s32[16,1,2]{2,1,0:T(1,128)}), s32[16,1,2]{2,1,0:T(1,128)S(1)}, u32[]{:S(2)}, u32[]{:S(2)}) async-start(s32[16,1,2]{2,1,0:T(1,128)} %bitcast.24), calls=%async_computation | async-start | bytes 16384 | tf_op jit(solution)/shard_map/all_to_all | solution.py:85
  25.2 21.2 %all-to-all-start.2 = ((bf16[16,2,128]{2,1,0:T(2,128)(2,1)}), bf16[16,2,128]{2,1,0:T(2,128)(2,1)S(1)}, u32[]{:S(2)}, u32[]{:S(2)}) async-start(bf16[16,2,128]{2,1,0:T(2,128)(2,1)} %broadcast_select_fusion.1), calls=%async_computation.2 | async-start | bytes 16384 | tf_op jit(solution)/shard_map/all_to_all | solution.py:89
  46.4 9.9 %copy-start = (s32[2,512]{1,0:T(2,128)S(1)}, s32[2,512]{1,0:T(2,128)}, u32[]{:S(2)}) copy-start(s32[2,512]{1,0:T(2,128)} %param.15) | copy-start | bytes 12292
  46.4 9.9 %copy-start.1 = (bf16[2,512]{1,0:T(2,128)(2,1)S(1)}, bf16[2,512]{1,0:T(2,128)(2,1)}, u32[]{:S(2)}) copy-start(bf16[2,512]{1,0:T(2,128)(2,1)} %param.14) | copy-start | bytes 6148
  46.4 9.9 %copy-start.2 = (s32[2]{0:T(128)S(1)}, s32[2]{0:T(128)}, u32[]{:S(2)}) copy-start(s32[2]{0:T(128)} %param.16) | copy-start | bytes 28
  46.4 10.7 %copy-start.3 = (s32[2,8]{1,0:T(2,128)S(1)}, s32[2,8]{1,0:T(2,128)}, u32[]{:S(2)}) copy-start(s32[2,8]{1,0:T(2,128)} %param.21) | copy-start | bytes 196
  46.4 244.6 %all-to-all-start.1 = ((bf16[16,2,128,1280]{3,2,1,0:T(8,128)(2,1)}), bf16[16,2,128,1280]{3,2,1,0:T(8,128)(2,1)}, u32[]{:S(2)}, u32[]{:S(2)}) async-start(bf16[16,2,128,1280]{3,2,1,0:T(8,128)(2,1)} %broadcast_select_fusion), calls=%async_computation.1 | async-start | bytes 20971520 | tf_op jit(solution)/shard_map/all_to_all | solution.py:88
  56.2 35.1 %collective-permute-start = (bf16[2,512,1280]{2,1,0:T(8,128)(2,1)}, bf16[2,512,1280]{2,1,0:T(8,128)(2,1)}, u32[]{:S(2)}, u32[]{:S(2)}) collective-permute-start(bf16[2,512,1280]{2,1,0:T(8,128)(2,1)} %param.13), channel_id=1, source_target_pairs={{0,16},{16,32},{32,48},{48,64},{64,80},{80,96},{96,112},{112,128},... | collective-permute-start | bytes 7864328 | tf_op jit(solution)/shard_map/ppermute | solution.py:9
  56.4 31.3 %collective-permute-start.1 = (bf16[2,512]{1,0:T(2,128)(2,1)S(1)}, bf16[2,512]{1,0:T(2,128)(2,1)S(1)}, u32[]{:S(2)}, u32[]{:S(2)}) collective-permute-start(bf16[2,512]{1,0:T(2,128)(2,1)S(1)} %get-tuple-element.273), channel_id=1, source_target_pairs={{0,16},{16,32},{32,48},{48,64},{64,80},{80,96},{96,112},{112,128},... | collective-permute-start | bytes 6152 | tf_op jit(solution)/shard_map/ppermute | solution.py:9
  87.6 3.0 collective-permute-start.3
  91.2 34.4 %collective-permute-start.2 = (bf16[2,512,1280]{2,1,0:T(8,128)(2,1)}, bf16[2,512,1280]{2,1,0:T(8,128)(2,1)}, u32[]{:S(2)}, u32[]{:S(2)}) collective-permute-start(bf16[2,512,1280]{2,1,0:T(8,128)(2,1)} %collective-permute-done), channel_id=1, source_target_pairs={{0,16},{16,32},{32,48},{48,64},{64,80},{80,96},{96,112},{112,128},... | collective-permute-start | bytes 7864328 | tf_op jit(solution)/shard_map/ppermute | solution.py:9
where the time goes:
time: 328 us; the launch traced here: 327 us
  waiting for transfers between devices  173 us (53%)
  matrix products  68.5 us (21%)
  local copies, waits for them, and re-layouts  44.3 us (14%)
  starting transfers between devices  26.2 us (8%)
  other arithmetic  14 us (4%)
    all_to_all x1, waiting for transfers between devices, fetch_hits(): lax.all_to_all(rows, 'pb', split_axis=0, concat_axis=0, tiled=True)  131 us
    dot_general x5, matrix products, diagonal_band(): jnp.dot(flat, diagonal_table(target_rows), precision=lax.Precision.HIGHES...  40.1 us
    ppermute x4, waiting for transfers between devices, passed_along(): lax.ppermute(value, axis, [(i, (i + by) % peers) for i in range(peers)])  33.4 us
    dot_general x4, matrix products, one_group(): jnp.einsum('kid,tjd->tkij', query_tiles, rows, preferred_element_type=jnp...  20.2 us
    reshape x5, local copies, waits for them, and re-layouts, diagonal_band(): flat = scores.reshape(leading + (blocks, target_rows * target_rows))  13.3 us
    all_to_all x1, starting transfers between devices, fetch_hits(): lax.all_to_all(requests, 'pb', split_axis=0, concat_axis=0, tiled=True)  11.2 us
    select_n x2, other arithmetic, fetch_hits(): rows = jnp.take(targets, wanted, axis=0)  10.2 us
    all_to_all x1, starting transfers between devices, fetch_hits(): lax.all_to_all(rows, 'pb', split_axis=0, concat_axis=0, tiled=True)  9.76 us
  transfers between devices with their start and end apart: 7, of which 4 were waited for; matrix products, arithmetic and copies ran while one was open for 27% of the time, Pallas kernels for 0%

commit v1 on v0

v1 whole, which is shorter than its diff:
```python
import functools

import jax
import jax.numpy as jnp
from jax import lax
from jax.experimental import pallas as pl
from jax.experimental.pallas import tpu as pltpu
from jax.sharding import PartitionSpec as P

MESH = pl.DeviceIdType.MESH
LANES = 128
NZ = 8
PEERS = NZ - 1
CHUNKS = 4


def weights_of(scale, mask, length):
    position = jnp.arange(scale.shape[1], dtype=jnp.int32)
    live = (mask == 1) & (position[None, :] < length[:, None])
    return jnp.where(live, scale, jnp.zeros_like(scale)).astype(jnp.float32)


def kernel(
    q_hbm, t_hbm, wt_in, wq_in, h_in, band_ref, resc_ref,
    qin, tin, ts, tall, qs, qr, qb, wt, wq, wqs, hv, hs, qwb, qwbb, sbuf, psum, prec, bo,
    in_sem, own_sem, t_send, t_recv, q_send, q_recv, y_send, y_recv, s2_send, s2_recv, s1_send, s1_recv,
    w_send, w_recv, m_send, m_recv, p_send, p_recv,
):
    n_db = lax.axis_size("db")
    db = lax.axis_index("db")
    pb = lax.axis_index("pb")
    z = pb // 2
    yh = lax.rem(pb, 2)
    core = lax.rem(db, 2)
    mate = db + 1 - 2 * core
    depth = ts.shape[2]
    half = qs.shape[3]

    def zdev(k):
        return (db, k * 2 + yh)

    def step_of(j):
        near = j // 2 + 1
        return jnp.where(lax.rem(j, 2) == 0, near, NZ - near)

    def to(j):
        return lax.rem(z + step_of(j), NZ)

    def frm(j):
        return lax.rem(z - step_of(j) + NZ, NZ)

    y_dev = (db, pb + 1 - 2 * yh)
    core_dev = (mate, pb)

    def shifted(by):
        return (lax.rem(db + by + n_db, n_db), pb)

    def remote(src, dst, send, recv, dev):
        return pltpu.make_async_remote_copy(
            src_ref=src, dst_ref=dst, send_sem=send, recv_sem=recv, device_id=dev, device_id_type=MESH
        )

    t_loads = [pltpu.make_async_copy(t_hbm.at[b], tin.at[b], in_sem.at[b]) for b in range(8)]
    q_loads = [pltpu.make_async_copy(q_hbm.at[k], qin.at[k], in_sem.at[8 + k]) for k in range(2)]
    for copy in t_loads + q_loads:
        copy.start()

    barrier = pltpu.get_barrier_semaphore()

    def greet(j, _):
        pl.semaphore_signal(barrier, inc=1, device_id=zdev(frm(j)), device_id_type=MESH)
        return 0

    lax.fori_loop(0, PEERS, greet, 0)
    for dev in (y_dev, core_dev, shifted(-1), shifted(-2)):
        pl.semaphore_signal(barrier, inc=1, device_id=dev, device_id_type=MESH)
    pl.semaphore_wait(barrier, PEERS + 4)

    s2 = [remote(q_hbm.at[k], qb.at[1, k], s2_send.at[k], s2_recv.at[k], shifted(2)) for k in range(2)]
    s1_even = [remote(q_hbm.at[k], qb.at[0, k], s1_send.at[k], s1_recv.at[k], core_dev) for k in range(2)]
    s1_odd = [remote(qb.at[1, k], qb.at[0, k], s1_send.at[k], s1_recv.at[k], core_dev) for k in range(2)]
    for copy in s2:
        copy.start()

    @pl.when(core == 0)
    def _():
        for copy in s1_even:
            copy.start()

    shift_w = [
        remote(wq_in, wqs.at[0], m_send.at[0], m_recv.at[0], shifted(1)),
        remote(wq_in, wqs.at[1], m_send.at[1], m_recv.at[1], shifted(2)),
    ]
    for copy in shift_w:
        copy.start()

    def small(j):
        dev = zdev(to(j))
        return [
            remote(wt_in, wt.at[z], w_send.at[0, j], w_recv.at[0, j], dev),
            remote(wq_in, wq.at[z], w_send.at[1, j], w_recv.at[1, j], dev),
            remote(h_in, hv.at[z], w_send.at[2, j], w_recv.at[2, j], dev),
        ]

    def start_small(j, _):
        for copy in small(j):
            copy.start()
        return 0

    lax.fori_loop(0, PEERS, start_small, 0)
    own_small = [
        pltpu.make_async_copy(wt_in, wt.at[z], own_sem.at[0]),
        pltpu.make_async_copy(wq_in, wq.at[z], own_sem.at[1]),
        pltpu.make_async_copy(h_in, hv.at[z], own_sem.at[2]),
    ]
    for copy in own_small:
        copy.start()

    flip = (
        lax.broadcasted_iota(jnp.int32, (LANES, LANES), 0) + lax.broadcasted_iota(jnp.int32, (LANES, LANES), 1)
        == LANES - 1
    ).astype(jnp.float32).astype(jnp.bfloat16)

    def t_copy(g, j):
        k = to(j)
        return remote(
            ts.at[k, pl.ds(2 * g, 2)], tall.at[z, pl.ds(2 * g, 2)], t_send.at[g, j], t_recv.at[g, j], zdev(k)
        )

    for copy in t_loads:
        copy.wait()

    def send_targets(g, _):
        for b in range(2):
            turned = jnp.dot(tin[2 * g + b].T, flip, preferred_element_type=jnp.float32).astype(jnp.bfloat16)
            ts[:, 2 * g + b] = turned.reshape(NZ, depth, LANES)

        def go(j, _):
            t_copy(g, j).start()
            return 0

        lax.fori_loop(0, PEERS, go, 0)
        return 0

    lax.fori_loop(0, 4, send_targets, 0)
    own_t = pltpu.make_async_copy(ts.at[z], tall.at[z], own_sem.at[3])
    own_t.start()

    for copy in q_loads:
        copy.wait()

    def q_copy(c, j):
        k = to(j)
        return remote(qs.at[k, c], qr.at[z, c], q_send.at[c, j], q_recv.at[c, j], zdev(k))

    def start_chunk(c):
        def go(j, _):
            q_copy(c, j).start()
            return 0

        lax.fori_loop(0, PEERS, go, 0)

    def turn_queries(c, _):
        rows = pl.ds(pl.multiple_of(lax.rem(c, 2) * half, half), half)
        turned = qin[c // 2, rows, :].T
        qs[:, c] = turned.reshape(NZ, depth, half)

        @pl.when(c == 0)
        def _():
            start_chunk(0)

        return 0

    lax.fori_loop(0, CHUNKS, turn_queries, 0)
    own_q = pltpu.make_async_copy(qs.at[z], qr.at[z], own_sem.at[4])
    own_q.start()

    def wait_small(j, _):
        for copy in small(j):
            copy.wait()
        return 0

    lax.fori_loop(0, PEERS, wait_small, 0)
    for copy in own_small:
        copy.wait()
    to_scalars = pltpu.make_async_copy(hv, hs, own_sem.at[5])
    to_scalars.start()
    for copy in shift_w:
        copy.wait()
    y_small = remote(wt.at[pl.ds(0, NZ)], wt.at[pl.ds(NZ, NZ)], m_send.at[2], m_recv.at[2], y_dev)
    y_small.start()

    def spread(row):
        return jnp.broadcast_to(row, (LANES, LANES)).T

    def spread_all(i, _):
        for m in range(8):
            rows = pl.ds((m % 4) * LANES, LANES)
            qwb[2 * i + m // 4, rows, :] = spread(wq[i, m : m + 1, :])
        return 0

    lax.fori_loop(0, NZ, spread_all, 0)

    def spread_shift(i, _):
        for m in range(8):
            rows = pl.ds((m % 4) * LANES, LANES)
            qwbb[2 * i + m // 4, rows, :] = spread(wqs[i, m : m + 1, :])
        return 0

    lax.fori_loop(0, 2, spread_shift, 0)

    def y_copy(i, src):
        return remote(tall.at[src], tall.at[NZ + src], y_send.at[i], y_recv.at[i], y_dev)

    own_t.wait()
    y_copy(PEERS, z).start()

    def pass_on(j, _):
        for g in range(4):
            t_copy(g, j).wait_recv()
        y_copy(j, frm(j)).start()
        return 0

    lax.fori_loop(0, PEERS, pass_on, 0)
    start_chunk(1)

    low = lax.broadcasted_iota(jnp.int32, (LANES, LANES), 1) >= lax.broadcasted_iota(jnp.int32, (LANES, LANES), 0)

    def diagonals(x):
        y = pltpu.roll(x, 0, 1, stride=1, stride_axis=0)
        lower = jnp.where(low, y, 0.0).reshape(LANES // 8, 8, LANES)
        upper = jnp.where(low, 0.0, y).reshape(LANES // 8, 8, LANES)
        return jnp.sum(lower, axis=0), jnp.sum(upper, axis=0)

    def row_sum(v):
        return jnp.sum(v, axis=0, keepdims=True)

    for k in range(2):
        s2[k].wait_recv()

    @pl.when(core == 1)
    def _():
        for copy in s1_odd:
            copy.start()

    def bands(s, k):
        def pair(p, _):
            rhs = jnp.concatenate(
                [ts[:, 2 * p].reshape(NZ * depth, LANES), ts[:, 2 * p + 1].reshape(NZ * depth, LANES)], axis=1
            )
            sbuf[...] = jnp.dot(qb[s, k], rhs, preferred_element_type=jnp.float32)
            for u in range(2):
                w8 = wt_in[2 * p + u]
                wrow = jnp.broadcast_to(w8[None], (LANES // 8, 8, LANES)).reshape(LANES, LANES)
                row = (s * 8 + 2 * p + u) * 2 + k
                carry = jnp.zeros((8, LANES), jnp.float32)
                for m in range(4):
                    rows = pl.ds(m * LANES, LANES)
                    x = sbuf[rows, u * LANES : (u + 1) * LANES] * qwbb[2 * s + k, rows, :] * wrow
                    lower, upper = diagonals(x)
                    bo[m, pl.ds(row, 1), :] = row_sum(carry + lower)
                    carry = upper
                bo[4, pl.ds(row, 1), :] = row_sum(carry)
            return 0

        lax.fori_loop(0, 4, pair, 0)

    lax.fori_loop(0, 2, lambda k, c: (bands(1, k), c)[1], 0)
    for k in range(2):
        s1_even[k].wait_recv()
    lax.fori_loop(0, 2, lambda k, c: (bands(0, k), c)[1], 0)

    def scores(segments):
        g = jnp.concatenate(segments, axis=1)
        return g + pltpu.roll(g, 1, 1)

    band_ref[...] = scores([bo[m] for m in range(5)])

    own_q.wait()
    to_scalars.wait()
    y_small.wait()
    psum[...] = jnp.zeros_like(psum)

    def wait_y(j, _):
        y_copy(j, frm(j)).wait()
        return 0

    lax.fori_loop(0, PEERS, wait_y, 0)
    y_copy(PEERS, z).wait()

    def chunk(c, _):
        def arrived(j, _):
            q_copy(c, j).wait_recv()
            return 0

        lax.fori_loop(0, PEERS, arrived, 0)

        @pl.when(c < CHUNKS - 2)
        def _():
            start_chunk(c + 2)

        tile, part = c // 2, lax.rem(c, 2)
        first = pl.multiple_of(part * half, half)

        def query(zq, _):
            lhs = qr[zq, c].T
            for pair in range(4):
                where = []
                for u in range(2):
                    hit = hs[zq, tile, 2 * pair + u]
                    owner, block = hit // 8, lax.rem(hit, 8)
                    other = jnp.where(lax.rem(owner, 2) == yh, 0, NZ)
                    where.append((other + owner // 2, block))
                rhs = jnp.concatenate([tall[o, b] for o, b in where], axis=1)
                s = jnp.dot(lhs, rhs, preferred_element_type=jnp.float32)
                for u in range(2):
                    o, b = where[u]
                    wrow = jnp.broadcast_to(wt[o, b][None], (LANES // 8, 8, LANES)).reshape(LANES, LANES)
                    row = tile * 8 + 2 * pair + u
                    carry = jnp.zeros((8, LANES), jnp.float32)
                    for m in range(2):
                        weight = qwb[2 * zq + tile, pl.ds(first + m * LANES, LANES), :]
                        x = s[m * LANES : (m + 1) * LANES, u * LANES : (u + 1) * LANES] * weight * wrow
                        lower, upper = diagonals(x)
                        psum[zq, 2 * part + m, pl.ds(row, 1), :] += row_sum(carry + lower)
                        carry = upper
                    psum[zq, 2 * part + 2, pl.ds(row, 1), :] += row_sum(carry)
            return 0

        lax.fori_loop(0, NZ, query, 0)
        return 0

    lax.fori_loop(0, CHUNKS, chunk, 0)

    def p_copy(j):
        k = to(j)
        return remote(psum.at[k], prec.at[z], p_send.at[j], p_recv.at[j], zdev(k))

    def start_p(j, _):
        p_copy(j).start()
        return 0

    lax.fori_loop(0, PEERS, start_p, 0)
    prec[z] = psum[z]

    def sent(j, _):
        for g in range(4):
            t_copy(g, j).wait_send()
        for c in range(CHUNKS):
            q_copy(c, j).wait_send()
        return 0

    lax.fori_loop(0, PEERS, sent, 0)
    for k in range(2):
        s2[k].wait_send()
        s1_even[k].wait_send()

    def wait_p(j, _):
        p_copy(j).wait()
        return 0

    lax.fori_loop(0, PEERS, wait_p, 0)
    total = prec[0]
    for k in range(1, NZ):
        total = total + prec[k]
    b = scores([total[m] for m in range(5)])
    mean = jnp.sum(jnp.maximum(b, 0.0), axis=1, keepdims=True) / (5 * LANES)
    resc_ref[...] = jnp.broadcast_to(mean, resc_ref.shape)


def shards(queries, query_scale, query_mask, query_len, targets, target_scale, target_mask, target_len, hit_ids):
    tiles, rows, width = queries.shape
    blocks, cols, _ = targets.shape
    hits = hit_ids.shape[1]
    depth = width // NZ
    half = rows // 2
    wq = weights_of(query_scale, query_mask, query_len).reshape(tiles * rows // LANES, LANES)
    wt = weights_of(target_scale, target_mask, target_len)[:, ::-1]
    wt = jnp.broadcast_to(wt[:, None, :], (blocks, 8, cols))
    group = lax.axis_size("pb") * blocks
    listed = jnp.zeros((8, LANES), jnp.int32).at[:tiles, :hits].set(hit_ids % group)
    vmem = functools.partial(pltpu.VMEM)
    dma = pltpu.SemaphoreType.DMA
    bf, f32 = jnp.bfloat16, jnp.float32
    band, resc = pl.pallas_call(
        kernel,
        out_shape=(
            jax.ShapeDtypeStruct((2 * blocks * tiles, rows + cols), f32),
            jax.ShapeDtypeStruct((tiles * hits, LANES), f32),
        ),
        in_specs=[pl.BlockSpec(memory_space=pl.ANY)] * 2 + [pl.BlockSpec(memory_space=pltpu.VMEM)] * 3,
        out_specs=(pl.BlockSpec(memory_space=pltpu.VMEM),) * 2,
        scratch_shapes=[
            vmem((tiles, rows, width), bf),
            vmem((blocks, cols, width), bf),
            vmem((NZ, blocks, depth, cols), bf),
            vmem((2 * NZ, blocks, depth, cols), bf),
            vmem((NZ, CHUNKS, depth, half), bf),
            vmem((NZ, CHUNKS, depth, half), bf),
            vmem((2, tiles, rows, width), bf),
            vmem((2 * NZ, blocks, 8, cols), f32),
            vmem((NZ, 8, LANES), f32),
            vmem((2, 8, LANES), f32),
            vmem((NZ, 8, LANES), jnp.int32),
            pltpu.SMEM((NZ, 8, LANES), jnp.int32),
            vmem((NZ * tiles, rows, LANES), f32),
            vmem((2 * tiles, rows, LANES), f32),
            vmem((rows, 2 * LANES), f32),
            vmem((NZ, 5, tiles * hits, LANES), f32),
            vmem((NZ, 5, tiles * hits, LANES), f32),
            vmem((5, 2 * blocks * tiles, LANES), f32),
            dma((10,)),
            dma((6,)),
            dma((4, PEERS)), dma((4, PEERS)),
            dma((CHUNKS, PEERS)), dma((CHUNKS, PEERS)),
            dma((NZ,)), dma((NZ,)),
            dma((2,)), dma((2,)),
            dma((2,)), dma((2,)),
            dma((3, PEERS)), dma((3, PEERS)),
            dma((3,)), dma((3,)),
            dma((PEERS,)), dma((PEERS,)),
        ],
        compiler_params=pltpu.CompilerParams(
            collective_id=0, has_side_effects=True, vmem_limit_bytes=56 * 1024 * 1024
        ),
    )(queries, targets, wt, wq, listed)
    return band.reshape(2, blocks, tiles, rows + cols), resc[:, 0].reshape(tiles, hits)


def solution(mesh):
    in_specs = (
        P(("db", "pb"), None, None),
        P(("db", "pb"), None),
        P(("db", "pb"), None),
        P(("db", "pb")),
        P(("db", "pb"), None, None),
        P(("db", "pb"), None),
        P(("db", "pb"), None),
        P(("db", "pb")),
        P(("db", "pb"), None),
    )
    out_specs = (P(None, ("db", "pb"), None, None), P(("db", "pb"), None))
    return jax.shard_map(shards, mesh=mesh, in_specs=in_specs, out_specs=out_specs, check_vma=False)
```

time: 328 us -> 186 us (0.57)
  Pallas kernels: 0 us -> 177 us
  waiting for transfers between devices: 173 us -> 0 us
  matrix products: 68.5 us -> 0 us
  local copies, waits for them, and re-layouts: 44.3 us -> 4.92 us
  starting transfers between devices: 26.2 us -> 0 us
  other arithmetic: 14 us -> 2.25 us
    pallas_call x0 -> x1, Pallas kernels: none -> 177 us  [shards(): pl.pallas_call(kernel, out_shape=(jax.ShapeDtypeStruct((2 * blocks * tile...]
    all_to_all x3 -> x0, waiting for transfers between devices: 140 us -> none  [the longest x1 131 us: fetch_hits(): lax.all_to_all(rows, 'pb', split_axis=0, concat_axis=0, tiled=True)]
    dot_general x10 -> x0, matrix products: 68.5 us -> none  [the longest x5 40.1 us: diagonal_band(): jnp.dot(flat, diagonal_table(target_rows), precision=lax.Precision.HIGHES...]
    ppermute x4 -> x0, waiting for transfers between devices: 33.4 us -> none  [passed_along(): lax.ppermute(value, axis, [(i, (i + by) % peers) for i in range(peers)])]
    all_to_all x3 -> x0, starting transfers between devices: 24.4 us -> none  [the longest x1 11.2 us: fetch_hits(): lax.all_to_all(requests, 'pb', split_axis=0, concat_axis=0, tiled=True)]
    gather x4 -> x0, local copies, waits for them, and re-layouts: 15.9 us -> none  [the longest x1 7.55 us: fetch_hits(): rows = jnp.take(targets, wanted, axis=0)]
    mul x5 -> x0, local copies, waits for them, and re-layouts: 13 us -> none  [the longest x4 7.62 us: one_group(): raw * query_wf[None, :, :, None]]
    reshape x12 -> x2, local copies, waits for them, and re-layouts: 14.2 us -> 2.17 us  [the longest x1 1.57 us: shards(): band.reshape(2, blocks, tiles, rows + cols)]
  transfers between devices with their start and end apart: 7 -> 0, of which waited for: 4 -> 0; matrix products, arithmetic and copies ran while one was open for 27% -> 0% of each run, Pallas kernels for 0% -> 0%
where the time goes in v1:
time: 186 us; the launch traced here: 184 us
  Pallas kernels  177 us (95%)
  local copies, waits for them, and re-layouts  4.92 us (3%)
  other arithmetic  2.25 us (1%)
    pallas_call x1, Pallas kernels, shards(): pl.pallas_call(kernel, out_shape=(jax.ShapeDtypeStruct((2 * blocks * tile...  177 us

profile of v1, /device:TPU:6, one launch (start us, length us, event | category | flops | bytes accessed | tf_op | source)
XLA Modules:
  0.0 184.3 jit_solution(15175513171213747920)
XLA Ops:
  0.6 0.7 and_select_fusion.1
  1.3 0.6 scatter.4.h_in
  1.9 0.8 fusion.3
  2.7 0.6 reshape.50.wq_in
  3.3 0.8 fusion.2
  4.1 0.1 rev.3
  4.2 0.6 broadcast_in_dim.7.wt_in
  4.8 176.5 %shard_map.104 = (f32[32,640]{1,0:T(8,128)}, f32[16,128]{1,0:T(8,128)}) custom-call(bf16[2,512,1280]{2,1,0:T(8,128)(2,1)} %q_hbm.1, bf16[8,128,1280]{2,1,0:T(8,128)(2,1)} %t_hbm.1, f32[8,8,128]{2,1,0:T(8,128)} %broadcast_in_dim.7.wt_in, f32[8,128]{1,0:T(8,128)} %reshape.50.wq_in, s32[8,128]{1,0:T(8,128)} %scatter.4.h_in), custom_call_target="tpu_custom_call" | custom-call | tf_op jit(solution)/shard_map/pallas_call | solution.py:385
  181.3 1.6 reshape.48
  182.9 0.8 slice_reduce_fusion
  183.7 0.6 reshape_squeeze.3

commit v2 on v1

--- a/solution.py
+++ b/solution.py
@@ -1,5 +1,3 @@
-import functools
-
 import jax
 import jax.numpy as jnp
 from jax import lax
@@ -14,15 +12,9 @@
 CHUNKS = 4
 
 
-def weights_of(scale, mask, length):
-    position = jnp.arange(scale.shape[1], dtype=jnp.int32)
-    live = (mask == 1) & (position[None, :] < length[:, None])
-    return jnp.where(live, scale, jnp.zeros_like(scale)).astype(jnp.float32)
-
-
 def kernel(
-    q_hbm, t_hbm, wt_in, wq_in, h_in, band_ref, resc_ref,
-    qin, tin, ts, tall, qs, qr, qb, wt, wq, wqs, hv, hs, qwb, qwbb, sbuf, psum, prec, bo,
+    q_hbm, qsc, qmk, qln, t_hbm, tsc, tmk, tln, h_in, band_ref, resc_ref,
+    qin, tin, ts, tall, qs, qr, qb, wown, wp, wps, wt, hown, hv, hs, qwb, qwbb, sbuf, psum, prec, bo,
     in_sem, own_sem, t_send, t_recv, q_send, q_recv, y_send, y_recv, s2_send, s2_recv, s1_send, s1_recv,
     w_send, w_recv, m_send, m_recv, p_send, p_recv,
 ):
@@ -74,7 +66,55 @@
     lax.fori_loop(0, PEERS, greet, 0)
     for dev in (y_dev, core_dev, shifted(-1), shifted(-2)):
         pl.semaphore_signal(barrier, inc=1, device_id=dev, device_id_type=MESH)
+
+    flip = (
+        lax.broadcasted_iota(jnp.int32, (LANES, LANES), 0) + lax.broadcasted_iota(jnp.int32, (LANES, LANES), 1)
+        == LANES - 1
+    ).astype(jnp.float32).astype(jnp.bfloat16)
+    position = lax.broadcasted_iota(jnp.int32, (8, LANES), 1)
+    place = lax.broadcasted_iota(jnp.int32, (8, LANES), 0)
+    lengths = jnp.zeros((8, LANES), jnp.int32)
+    for b in range(8):
+        lengths = jnp.where(place == b, tln[b], lengths)
+    t_scale = tsc[...].astype(jnp.float32)
+    t_weight = jnp.where(tmk[...] == 1, jnp.where(position < lengths, t_scale, 0.0), 0.0)
+    t_weight = jnp.dot(t_weight.astype(jnp.bfloat16), flip, preferred_element_type=jnp.float32)
+    q_scale = qsc[...].astype(jnp.float32)
+    q_mask = qmk[...]
+    q_rows = []
+    for k in range(2):
+        for m in range(4):
+            cols = slice(m * LANES, (m + 1) * LANES)
+            at = lax.broadcasted_iota(jnp.int32, (1, LANES), 1) + m * LANES
+            kept = jnp.where(at < qln[k], q_scale[k : k + 1, cols], 0.0)
+            q_rows.append(jnp.where(q_mask[k : k + 1, cols] == 1, kept, 0.0))
+    wown[...] = jnp.concatenate([t_weight] + q_rows, axis=0).astype(jnp.bfloat16)
+    hown[...] = jnp.zeros_like(hown)
+    hown[0:2, 0:8] = h_in[...]
+
+    def turn_targets(g):
+        for b in range(2):
+            turned = jnp.dot(tin[2 * g + b].T, flip, preferred_element_type=jnp.float32).astype(jnp.bfloat16)
+            ts[:, 2 * g + b] = turned.reshape(NZ, depth, LANES)
+
+    def t_copy(g, j):
+        k = to(j)
+        return remote(
+            ts.at[k, pl.ds(2 * g, 2)], tall.at[z, pl.ds(2 * g, 2)], t_send.at[g, j], t_recv.at[g, j], zdev(k)
+        )
+
+    def start_targets(g):
+        def go(j, _):
+            t_copy(g, j).start()
+            return 0
+
+        lax.fori_loop(0, PEERS, go, 0)
+
+    t_loads[0].wait()
+    t_loads[1].wait()
+    turn_targets(0)
     pl.semaphore_wait(barrier, PEERS + 4)
+    start_targets(0)
 
     s2 = [remote(q_hbm.at[k], qb.at[1, k], s2_send.at[k], s2_recv.at[k], shifted(2)) for k in range(2)]
     s1_even = [remote(q_hbm.at[k], qb.at[0, k], s1_send.at[k], s1_recv.at[k], core_dev) for k in range(2)]
@@ -87,19 +127,15 @@
         for copy in s1_even:
             copy.start()
 
-    shift_w = [
-        remote(wq_in, wqs.at[0], m_send.at[0], m_recv.at[0], shifted(1)),
-        remote(wq_in, wqs.at[1], m_send.at[1], m_recv.at[1], shifted(2)),
-    ]
+    shift_w = [remote(wown, wps.at[i], m_send.at[i], m_recv.at[i], shifted(i + 1)) for i in range(2)]
     for copy in shift_w:
         copy.start()
 
     def small(j):
         dev = zdev(to(j))
         return [
-            remote(wt_in, wt.at[z], w_send.at[0, j], w_recv.at[0, j], dev),
-            remote(wq_in, wq.at[z], w_send.at[1, j], w_recv.at[1, j], dev),
-            remote(h_in, hv.at[z], w_send.at[2, j], w_recv.at[2, j], dev),
+            remote(wown, wp.at[z], w_send.at[0, j], w_recv.at[0, j], dev),
+            remote(hown, hv.at[z], w_send.at[1, j], w_recv.at[1, j], dev),
         ]
 
     def start_small(j, _):
@@ -109,40 +145,21 @@
 
     lax.fori_loop(0, PEERS, start_small, 0)
     own_small = [
-        pltpu.make_async_copy(wt_in, wt.at[z], own_sem.at[0]),
-        pltpu.make_async_copy(wq_in, wq.at[z], own_sem.at[1]),
-        pltpu.make_async_copy(h_in, hv.at[z], own_sem.at[2]),
+        pltpu.make_async_copy(wown, wp.at[z], own_sem.at[0]),
+        pltpu.make_async_copy(hown, hv.at[z], own_sem.at[1]),
     ]
     for copy in own_small:
         copy.start()
 
-    flip = (
-        lax.broadcasted_iota(jnp.int32, (LANES, LANES), 0) + lax.broadcasted_iota(jnp.int32, (LANES, LANES), 1)
-        == LANES - 1
-    ).astype(jnp.float32).astype(jnp.bfloat16)
-
-    def t_copy(g, j):
-        k = to(j)
-        return remote(
-            ts.at[k, pl.ds(2 * g, 2)], tall.at[z, pl.ds(2 * g, 2)], t_send.at[g, j], t_recv.at[g, j], zdev(k)
-        )
-
-    for copy in t_loads:
+    for copy in t_loads[2:]:
         copy.wait()
 
     def send_targets(g, _):
-        for b in range(2):
-            turned = jnp.dot(tin[2 * g + b].T, flip, preferred_element_type=jnp.float32).astype(jnp.bfloat16)
-            ts[:, 2 * g + b] = turned.reshape(NZ, depth, LANES)
-
-        def go(j, _):
-            t_copy(g, j).start()
-            return 0
-
-        lax.fori_loop(0, PEERS, go, 0)
-        return 0
-
-    lax.fori_loop(0, 4, send_targets, 0)
+        turn_targets(g)
+        start_targets(g)
+        return 0
+
+    lax.fori_loop(1, 4, send_targets, 0)
     own_t = pltpu.make_async_copy(ts.at[z], tall.at[z], own_sem.at[3])
     own_t.start()
 
@@ -187,24 +204,34 @@
     to_scalars.start()
     for copy in shift_w:
         copy.wait()
-    y_small = remote(wt.at[pl.ds(0, NZ)], wt.at[pl.ds(NZ, NZ)], m_send.at[2], m_recv.at[2], y_dev)
+    y_small = remote(wp.at[pl.ds(0, NZ)], wp.at[pl.ds(NZ, NZ)], m_send.at[2], m_recv.at[2], y_dev)
     y_small.start()
 
     def spread(row):
         return jnp.broadcast_to(row, (LANES, LANES)).T
 
     def spread_all(i, _):
+        w = wp[i].astype(jnp.float32)
         for m in range(8):
             rows = pl.ds((m % 4) * LANES, LANES)
-            qwb[2 * i + m // 4, rows, :] = spread(wq[i, m : m + 1, :])
+            qwb[2 * i + m // 4, rows, :] = spread(w[8 + m : 9 + m])
         return 0
 
     lax.fori_loop(0, NZ, spread_all, 0)
 
+    def widen(o, _):
+        w = wp[o].astype(jnp.float32)
+        for b in range(8):
+            wt[o, b] = jnp.broadcast_to(w[b : b + 1], (8, LANES))
+        return 0
+
+    lax.fori_loop(0, NZ, widen, 0)
+
     def spread_shift(i, _):
+        w = wps[i].astype(jnp.float32)
         for m in range(8):
             rows = pl.ds((m % 4) * LANES, LANES)
-            qwbb[2 * i + m // 4, rows, :] = spread(wqs[i, m : m + 1, :])
+            qwbb[2 * i + m // 4, rows, :] = spread(w[8 + m : 9 + m])
         return 0
 
     lax.fori_loop(0, 2, spread_shift, 0)
@@ -223,6 +250,16 @@
 
     lax.fori_loop(0, PEERS, pass_on, 0)
     start_chunk(1)
+
+    def chunk_arrived(c):
+        def go(j, _):
+            q_copy(c, j).wait_recv()
+            return 0
+
+        lax.fori_loop(0, PEERS, go, 0)
+
+    chunk_arrived(0)
+    start_chunk(2)
 
     low = lax.broadcasted_iota(jnp.int32, (LANES, LANES), 1) >= lax.broadcasted_iota(jnp.int32, (LANES, LANES), 0)
 
@@ -250,7 +287,7 @@
             )
             sbuf[...] = jnp.dot(qb[s, k], rhs, preferred_element_type=jnp.float32)
             for u in range(2):
-                w8 = wt_in[2 * p + u]
+                w8 = wt[z, 2 * p + u]
                 wrow = jnp.broadcast_to(w8[None], (LANES // 8, 8, LANES)).reshape(LANES, LANES)
                 row = (s * 8 + 2 * p + u) * 2 + k
                 carry = jnp.zeros((8, LANES), jnp.float32)
@@ -266,6 +303,8 @@
         lax.fori_loop(0, 4, pair, 0)
 
     lax.fori_loop(0, 2, lambda k, c: (bands(1, k), c)[1], 0)
+    chunk_arrived(1)
+    start_chunk(3)
     for k in range(2):
         s1_even[k].wait_recv()
     lax.fori_loop(0, 2, lambda k, c: (bands(0, k), c)[1], 0)
@@ -274,11 +313,15 @@
         g = jnp.concatenate(segments, axis=1)
         return g + pltpu.roll(g, 1, 1)
 
-    band_ref[...] = scores([bo[m] for m in range(5)])
+    band = scores([bo[m] for m in range(5)])
+    for s in range(2):
+        for t in range(8):
+            band_ref[s, t] = band[(s * 8 + t) * 2 : (s * 8 + t) * 2 + 2]
 
     own_q.wait()
     to_scalars.wait()
     y_small.wait()
+    lax.fori_loop(NZ, 2 * NZ, widen, 0)
     psum[...] = jnp.zeros_like(psum)
 
     def wait_y(j, _):
@@ -288,16 +331,30 @@
     lax.fori_loop(0, PEERS, wait_y, 0)
     y_copy(PEERS, z).wait()
 
+    def p_copy(part, j):
+        k = to(j)
+        tile, seg, count = ((0, 0, 5), (1, 0, 2), (1, 2, 3))[part]
+        return remote(
+            psum.at[k, tile, pl.ds(seg, count)], prec.at[z, tile, pl.ds(seg, count)],
+            p_send.at[part, j], p_recv.at[part, j], zdev(k),
+        )
+
+    def start_p(part):
+        def go(j, _):
+            p_copy(part, j).start()
+            return 0
+
+        lax.fori_loop(0, PEERS, go, 0)
+
     def chunk(c, _):
-        def arrived(j, _):
-            q_copy(c, j).wait_recv()
-            return 0
-
-        lax.fori_loop(0, PEERS, arrived, 0)
-
-        @pl.when(c < CHUNKS - 2)
+        @pl.when(c >= 2)
         def _():
-            start_chunk(c + 2)
+            chunk_arrived(c)
+
+        @pl.when(c == CHUNKS - 1)
+        def _():
+            start_p(0)
+            start_p(1)
 
         tile, part = c // 2, lax.rem(c, 2)
         first = pl.multiple_of(part * half, half)
@@ -307,7 +364,7 @@
             for pair in range(4):
                 where = []
                 for u in range(2):
-                    hit = hs[zq, tile, 2 * pair + u]
+                    hit = lax.rem(hs[zq, tile, 2 * pair + u], 2 * NZ * 8)
                     owner, block = hit // 8, lax.rem(hit, 8)
                     other = jnp.where(lax.rem(owner, 2) == yh, 0, NZ)
                     where.append((other + owner // 2, block))
@@ -316,15 +373,15 @@
                 for u in range(2):
                     o, b = where[u]
                     wrow = jnp.broadcast_to(wt[o, b][None], (LANES // 8, 8, LANES)).reshape(LANES, LANES)
-                    row = tile * 8 + 2 * pair + u
+                    row = 2 * pair + u
                     carry = jnp.zeros((8, LANES), jnp.float32)
                     for m in range(2):
                         weight = qwb[2 * zq + tile, pl.ds(first + m * LANES, LANES), :]
                         x = s[m * LANES : (m + 1) * LANES, u * LANES : (u + 1) * LANES] * weight * wrow
                         lower, upper = diagonals(x)
-                        psum[zq, 2 * part + m, pl.ds(row, 1), :] += row_sum(carry + lower)
+                        psum[zq, tile, 2 * part + m, row : row + 1, :] += row_sum(carry + lower)
                         carry = upper
-                    psum[zq, 2 * part + 2, pl.ds(row, 1), :] += row_sum(carry)
+                    psum[zq, tile, 2 * part + 2, row : row + 1, :] += row_sum(carry)
             return 0
 
         lax.fori_loop(0, NZ, query, 0)
@@ -332,15 +389,7 @@
 
     lax.fori_loop(0, CHUNKS, chunk, 0)
 
-    def p_copy(j):
-        k = to(j)
-        return remote(psum.at[k], prec.at[z], p_send.at[j], p_recv.at[j], zdev(k))
-
-    def start_p(j, _):
-        p_copy(j).start()
-        return 0
-
-    lax.fori_loop(0, PEERS, start_p, 0)
+    start_p(2)
     prec[z] = psum[z]
 
     def sent(j, _):
@@ -356,16 +405,19 @@
         s1_even[k].wait_send()
 
     def wait_p(j, _):
-        p_copy(j).wait()
+        for part in range(3):
+            p_copy(part, j).wait()
         return 0
 
     lax.fori_loop(0, PEERS, wait_p, 0)
     total = prec[0]
     for k in range(1, NZ):
         total = total + prec[k]
-    b = scores([total[m] for m in range(5)])
-    mean = jnp.sum(jnp.maximum(b, 0.0), axis=1, keepdims=True) / (5 * LANES)
-    resc_ref[...] = jnp.broadcast_to(mean, resc_ref.shape)
+    for tile in range(2):
+        b = scores([total[tile, m] for m in range(5)])
+        mean = jnp.sum(jnp.maximum(b, 0.0), axis=1, keepdims=True) / (5 * LANES)
+        line = jnp.sum(jnp.where(position == place, jnp.broadcast_to(mean, (8, LANES)), 0.0), axis=0, keepdims=True)
+        resc_ref[tile : tile + 1, :] = line[:, 0:8]
 
 
 def shards(queries, query_scale, query_mask, query_len, targets, target_scale, target_mask, target_len, hit_ids):
@@ -374,21 +426,18 @@
     hits = hit_ids.shape[1]
     depth = width // NZ
     half = rows // 2
-    wq = weights_of(query_scale, query_mask, query_len).reshape(tiles * rows // LANES, LANES)
-    wt = weights_of(target_scale, target_mask, target_len)[:, ::-1]
-    wt = jnp.broadcast_to(wt[:, None, :], (blocks, 8, cols))
-    group = lax.axis_size("pb") * blocks
-    listed = jnp.zeros((8, LANES), jnp.int32).at[:tiles, :hits].set(hit_ids % group)
-    vmem = functools.partial(pltpu.VMEM)
+    vmem = pltpu.VMEM
+    one = (pl.ANY, vmem, vmem, pltpu.SMEM)
+    spaces = one + one + (vmem,)
     dma = pltpu.SemaphoreType.DMA
     bf, f32 = jnp.bfloat16, jnp.float32
     band, resc = pl.pallas_call(
         kernel,
         out_shape=(
-            jax.ShapeDtypeStruct((2 * blocks * tiles, rows + cols), f32),
-            jax.ShapeDtypeStruct((tiles * hits, LANES), f32),
+            jax.ShapeDtypeStruct((2, blocks, tiles, rows + cols), f32),
+            jax.ShapeDtypeStruct((tiles, hits), f32),
         ),
-        in_specs=[pl.BlockSpec(memory_space=pl.ANY)] * 2 + [pl.BlockSpec(memory_space=pltpu.VMEM)] * 3,
+        in_specs=[pl.BlockSpec(memory_space=m) for m in spaces],
         out_specs=(pl.BlockSpec(memory_space=pltpu.VMEM),) * 2,
         scratch_shapes=[
             vmem((tiles, rows, width), bf),
@@ -398,16 +447,18 @@
             vmem((NZ, CHUNKS, depth, half), bf),
             vmem((NZ, CHUNKS, depth, half), bf),
             vmem((2, tiles, rows, width), bf),
+            vmem((16, LANES), bf),
+            vmem((2 * NZ, 16, LANES), bf),
+            vmem((2, 16, LANES), bf),
             vmem((2 * NZ, blocks, 8, cols), f32),
-            vmem((NZ, 8, LANES), f32),
-            vmem((2, 8, LANES), f32),
+            vmem((8, LANES), jnp.int32),
             vmem((NZ, 8, LANES), jnp.int32),
             pltpu.SMEM((NZ, 8, LANES), jnp.int32),
             vmem((NZ * tiles, rows, LANES), f32),
             vmem((2 * tiles, rows, LANES), f32),
             vmem((rows, 2 * LANES), f32),
-            vmem((NZ, 5, tiles * hits, LANES), f32),
-            vmem((NZ, 5, tiles * hits, LANES), f32),
+            vmem((NZ, tiles, 5, hits, LANES), f32),
+            vmem((NZ, tiles, 5, hits, LANES), f32),
             vmem((5, 2 * blocks * tiles, LANES), f32),
             dma((10,)),
             dma((6,)),
@@ -416,15 +467,15 @@
             dma((NZ,)), dma((NZ,)),
             dma((2,)), dma((2,)),
             dma((2,)), dma((2,)),
+            dma((2, PEERS)), dma((2, PEERS)),
+            dma((3,)), dma((3,)),
             dma((3, PEERS)), dma((3, PEERS)),
-            dma((3,)), dma((3,)),
-            dma((PEERS,)), dma((PEERS,)),
         ],
         compiler_params=pltpu.CompilerParams(
             collective_id=0, has_side_effects=True, vmem_limit_bytes=56 * 1024 * 1024
         ),
-    )(queries, targets, wt, wq, listed)
-    return band.reshape(2, blocks, tiles, rows + cols), resc[:, 0].reshape(tiles, hits)
+    )(queries, query_scale, query_mask, query_len, targets, target_scale, target_mask, target_len, hit_ids)
+    return band, resc
 
 
 def solution(mesh):

time: 186 us -> 158 us (0.85)
  Pallas kernels: 177 us -> 153 us
  other arithmetic: 2.25 us -> 0 us
  local copies, waits for them, and re-layouts: 4.92 us -> 2.76 us
    pallas_call x1, Pallas kernels: 177 us -> 153 us  [shards(): pl.pallas_call(kernel, out_shape=(jax.ShapeDtypeStruct((2, blocks, tiles,...]
    unnamed x0 -> x2, local copies, waits for them, and re-layouts: none -> 2.76 us
    reshape x2 -> x0, local copies, waits for them, and re-layouts: 2.17 us -> none  [the longest x1 1.57 us: shards(): band.reshape(2, blocks, tiles, rows + cols)]
where the time goes in v2:
time: 158 us; the launch traced here: 156 us
  Pallas kernels  153 us (97%)
  local copies, waits for them, and re-layouts  2.76 us (2%)
    pallas_call x1, Pallas kernels, shards(): pl.pallas_call(kernel, out_shape=(jax.ShapeDtypeStruct((2, blocks, tiles,...  153 us

profile of v2, /device:TPU:6, one launch (start us, length us, event | category | flops | bytes accessed | tf_op | source)
XLA Modules:
  0.0 156.2 jit_solution(18243615889472364909)
XLA Ops:
  0.6 152.8 %shard_map.104 = (f32[2,8,2,640]{3,2,1,0:T(2,128)}, f32[2,8]{1,0:T(2,128)}) custom-call(bf16[2,512,1280]{2,1,0:T(8,128)(2,1)} %q_hbm.1, bf16[2,512]{1,0:T(2,128)(2,1)} %qsc.1, s32[2,512]{1,0:T(2,128)} %qmk.1, s32[2]{0:T(128)} %qln.1, bf16[8,128,1280]{2,1,0:T(8,128)(2,1)} %t_hbm.1, bf16[8,128]{1,0:T(8,128)(2,1)} %tsc.1, s32[8,128]{1,0:T(8,128)} %tmk.1, ...), custom_call_target="tpu_custom_call" | custom-call | tf_op jit(solution)/shard_map/pallas_call | solution.py:434
  153.4 1.5 copy.13
  155.0 1.2 copy.14

commit v3 on v2

--- a/solution.py
+++ b/solution.py
@@ -9,14 +9,15 @@
 LANES = 128
 NZ = 8
 PEERS = NZ - 1
+AHEAD = 4
 CHUNKS = 4
 
 
 def kernel(
     q_hbm, qsc, qmk, qln, t_hbm, tsc, tmk, tln, h_in, band_ref, resc_ref,
-    qin, tin, ts, tall, qs, qr, qb, wown, wp, wps, wt, hown, hv, hs, qwb, qwbb, sbuf, psum, prec, bo,
+    qin, tin, ts, tall, qs, qr, qb, wown, wp, wps, wt, hown, hv, hs, qwb, qwbb, sbuf, psum, prec, bo, via,
     in_sem, own_sem, t_send, t_recv, q_send, q_recv, y_send, y_recv, s2_send, s2_recv, s1_send, s1_recv,
-    w_send, w_recv, m_send, m_recv, p_send, p_recv,
+    w_send, w_recv, m_send, m_recv, p_send, p_recv, v_send, v_recv,
 ):
     n_db = lax.axis_size("db")
     db = lax.axis_index("db")
@@ -25,6 +26,8 @@
     yh = lax.rem(pb, 2)
     core = lax.rem(db, 2)
     mate = db + 1 - 2 * core
+    last_x = lax.rem(db, 8) >= 6
+    first_x = lax.rem(db, 8) < 2
     depth = ts.shape[2]
     half = qs.shape[3]
 
@@ -66,6 +69,14 @@
     lax.fori_loop(0, PEERS, greet, 0)
     for dev in (y_dev, core_dev, shifted(-1), shifted(-2)):
         pl.semaphore_signal(barrier, inc=1, device_id=dev, device_id_type=MESH)
+
+    @pl.when(last_x)
+    def _():
+        pl.semaphore_signal(barrier, inc=1, device_id=shifted(8), device_id_type=MESH)
+
+    @pl.when(first_x)
+    def _():
+        pl.semaphore_signal(barrier, inc=1, device_id=shifted(-10), device_id_type=MESH)
 
     flip = (
         lax.broadcasted_iota(jnp.int32, (LANES, LANES), 0) + lax.broadcasted_iota(jnp.int32, (LANES, LANES), 1)
@@ -113,19 +124,7 @@
     t_loads[0].wait()
     t_loads[1].wait()
     turn_targets(0)
-    pl.semaphore_wait(barrier, PEERS + 4)
-    start_targets(0)
-
-    s2 = [remote(q_hbm.at[k], qb.at[1, k], s2_send.at[k], s2_recv.at[k], shifted(2)) for k in range(2)]
-    s1_even = [remote(q_hbm.at[k], qb.at[0, k], s1_send.at[k], s1_recv.at[k], core_dev) for k in range(2)]
-    s1_odd = [remote(qb.at[1, k], qb.at[0, k], s1_send.at[k], s1_recv.at[k], core_dev) for k in range(2)]
-    for copy in s2:
-        copy.start()
-
-    @pl.when(core == 0)
-    def _():
-        for copy in s1_even:
-            copy.start()
+    pl.semaphore_wait(barrier, PEERS + 4 + jnp.where(last_x, 2, 0))
 
     shift_w = [remote(wown, wps.at[i], m_send.at[i], m_recv.at[i], shifted(i + 1)) for i in range(2)]
     for copy in shift_w:
@@ -151,12 +150,38 @@
     for copy in own_small:
         copy.start()
 
+    start_targets(0)
+
+    s2 = [remote(q_hbm.at[k], qb.at[1, k], s2_send.at[k], s2_recv.at[k], shifted(2)) for k in range(2)]
+    s1_even = [remote(q_hbm.at[k], qb.at[0, k], s1_send.at[k], s1_recv.at[k], core_dev) for k in range(2)]
+    s1_odd = [remote(qb.at[1, k], qb.at[0, k], s1_send.at[k], s1_recv.at[k], core_dev) for k in range(2)]
+    s2_first = remote(q_hbm.at[1], via, v_send.at[0], v_recv.at[0], shifted(8))
+    s2_then = remote(via, qb.at[1, 1], s2_send.at[1], s2_recv.at[1], shifted(10))
+    s2[0].start()
+
+    @pl.when(last_x)
+    def _():
+        s2_first.start()
+
+    @pl.when(jnp.logical_not(last_x))
+    def _():
+        s2[1].start()
+
+    @pl.when(core == 0)
+    def _():
+        for copy in s1_even:
+            copy.start()
+
     for copy in t_loads[2:]:
         copy.wait()
 
     def send_targets(g, _):
         turn_targets(g)
-        start_targets(g)
+
+        @pl.when(g < AHEAD)
+        def _():
+            start_targets(g)
+
         return 0
 
     lax.fori_loop(1, 4, send_targets, 0)
@@ -182,15 +207,50 @@
         turned = qin[c // 2, rows, :].T
         qs[:, c] = turned.reshape(NZ, depth, half)
 
-        @pl.when(c == 0)
+        @pl.when(c + 4 < AHEAD)
         def _():
-            start_chunk(0)
+            start_chunk(c)
 
         return 0
 
     lax.fori_loop(0, CHUNKS, turn_queries, 0)
     own_q = pltpu.make_async_copy(qs.at[z], qr.at[z], own_sem.at[4])
     own_q.start()
+
+    def y_copy(g, i, src):
+        part = pl.ds(2 * g, 2)
+        return remote(tall.at[src, part], tall.at[NZ + src, part], y_send.at[g, i], y_recv.at[g, i], y_dev)
+
+    own_t.wait()
+
+    def pass_on(g, _):
+        y_copy(g, PEERS, z).start()
+
+        def go(j, _):
+            t_copy(g, j).wait_recv()
+            y_copy(g, j, frm(j)).start()
+            later = g + AHEAD
+
+            @pl.when(later < 4)
+            def _():
+                t_copy(later, j).start()
+
+            @pl.when(jnp.logical_and(later >= 4, later < 8))
+            def _():
+                q_copy(later - 4, j).start()
+
+            return 0
+
+        lax.fori_loop(0, PEERS, go, 0)
+
+        @pl.when(jnp.logical_and(g == 0, last_x))
+        def _():
+            s2_first.wait()
+            s2_then.start()
+
+        return 0
+
+    lax.fori_loop(0, 4, pass_on, 0)
 
     def wait_small(j, _):
         for copy in small(j):
@@ -236,30 +296,20 @@
 
     lax.fori_loop(0, 2, spread_shift, 0)
 
-    def y_copy(i, src):
-        return remote(tall.at[src], tall.at[NZ + src], y_send.at[i], y_recv.at[i], y_dev)
-
-    own_t.wait()
-    y_copy(PEERS, z).start()
-
-    def pass_on(j, _):
-        for g in range(4):
-            t_copy(g, j).wait_recv()
-        y_copy(j, frm(j)).start()
-        return 0
-
-    lax.fori_loop(0, PEERS, pass_on, 0)
-    start_chunk(1)
-
     def chunk_arrived(c):
         def go(j, _):
             q_copy(c, j).wait_recv()
+            later = c + AHEAD
+
+            @pl.when(later < CHUNKS)
+            def _():
+                q_copy(later, j).start()
+
             return 0
 
         lax.fori_loop(0, PEERS, go, 0)
 
     chunk_arrived(0)
-    start_chunk(2)
 
     low = lax.broadcasted_iota(jnp.int32, (LANES, LANES), 1) >= lax.broadcasted_iota(jnp.int32, (LANES, LANES), 0)
 
@@ -304,7 +354,6 @@
 
     lax.fori_loop(0, 2, lambda k, c: (bands(1, k), c)[1], 0)
     chunk_arrived(1)
-    start_chunk(3)
     for k in range(2):
         s1_even[k].wait_recv()
     lax.fori_loop(0, 2, lambda k, c: (bands(0, k), c)[1], 0)
@@ -324,12 +373,16 @@
     lax.fori_loop(NZ, 2 * NZ, widen, 0)
     psum[...] = jnp.zeros_like(psum)
 
-    def wait_y(j, _):
-        y_copy(j, frm(j)).wait()
-        return 0
-
-    lax.fori_loop(0, PEERS, wait_y, 0)
-    y_copy(PEERS, z).wait()
+    def wait_y(g, _):
+        def go(j, _):
+            y_copy(g, j, frm(j)).wait()
+            return 0
+
+        lax.fori_loop(0, PEERS, go, 0)
+        y_copy(g, PEERS, z).wait()
+        return 0
+
+    lax.fori_loop(0, 4, wait_y, 0)
 
     def p_copy(part, j):
         k = to(j)
@@ -460,16 +513,18 @@
             vmem((NZ, tiles, 5, hits, LANES), f32),
             vmem((NZ, tiles, 5, hits, LANES), f32),
             vmem((5, 2 * blocks * tiles, LANES), f32),
+            vmem((rows, width), bf),
             dma((10,)),
             dma((6,)),
             dma((4, PEERS)), dma((4, PEERS)),
             dma((CHUNKS, PEERS)), dma((CHUNKS, PEERS)),
-            dma((NZ,)), dma((NZ,)),
+            dma((4, NZ)), dma((4, NZ)),
             dma((2,)), dma((2,)),
             dma((2,)), dma((2,)),
             dma((2, PEERS)), dma((2, PEERS)),
             dma((3,)), dma((3,)),
             dma((3, PEERS)), dma((3, PEERS)),
+            dma((1,)), dma((1,)),
         ],
         compiler_params=pltpu.CompilerParams(
             collective_id=0, has_side_effects=True, vmem_limit_bytes=56 * 1024 * 1024

time: 158 us -> 142 us (0.90)
  Pallas kernels: 153 us -> 138 us
    pallas_call x1, Pallas kernels: 153 us -> 138 us  [shards(): pl.pallas_call(kernel, out_shape=(jax.ShapeDtypeStruct((2, blocks, tiles,...]
where the time goes in v3:
time: 142 us; the launch traced here: 141 us
  Pallas kernels  138 us (97%)
  local copies, waits for them, and re-layouts  2.76 us (2%)
    pallas_call x1, Pallas kernels, shards(): pl.pallas_call(kernel, out_shape=(jax.ShapeDtypeStruct((2, blocks, tiles,...  138 us

profile of v3, /device:TPU:6, one launch (start us, length us, event | category | flops | bytes accessed | tf_op | source)
XLA Modules:
  0.0 141.2 jit_solution(18263479918021715811)
XLA Ops:
  0.6 137.8 %shard_map.104 = (f32[2,8,2,640]{3,2,1,0:T(2,128)}, f32[2,8]{1,0:T(2,128)}) custom-call(bf16[2,512,1280]{2,1,0:T(8,128)(2,1)} %q_hbm.1, bf16[2,512]{1,0:T(2,128)(2,1)} %qsc.1, s32[2,512]{1,0:T(2,128)} %qmk.1, s32[2]{0:T(128)} %qln.1, bf16[8,128,1280]{2,1,0:T(8,128)(2,1)} %t_hbm.1, bf16[8,128]{1,0:T(8,128)(2,1)} %tsc.1, s32[8,128]{1,0:T(8,128)} %tmk.1, ...), custom_call_target="tpu_custom_call" | custom-call | tf_op jit(solution)/shard_map/pallas_call | solution.py:487
  138.4 1.5 %copy.13 = f32[2,8,2,640]{3,2,1,0:T(2,128)} copy(f32[2,8,2,640]{3,2,1,0:T(2,128)} %get-tuple-element.4) | data formatting | bytes 163840
  140.0 1.2 copy.14

commit v4 on v3

--- a/solution.py
+++ b/solution.py
@@ -10,6 +10,8 @@
 NZ = 8
 PEERS = NZ - 1
 AHEAD = 4
+GROUPS = 2
+EACH = 8 // GROUPS
 CHUNKS = 4
 
 
@@ -35,8 +37,8 @@
         return (db, k * 2 + yh)
 
     def step_of(j):
-        near = j // 2 + 1
-        return jnp.where(lax.rem(j, 2) == 0, near, NZ - near)
+        far = NZ // 2 - (j + 1) // 2
+        return jnp.where(lax.rem(j, 2) == 0, far, NZ - far)
 
     def to(j):
         return lax.rem(z + step_of(j), NZ)
@@ -82,6 +84,31 @@
         lax.broadcasted_iota(jnp.int32, (LANES, LANES), 0) + lax.broadcasted_iota(jnp.int32, (LANES, LANES), 1)
         == LANES - 1
     ).astype(jnp.float32).astype(jnp.bfloat16)
+    def turn_targets(g):
+        for b in range(EACH):
+            turned = jnp.dot(tin[EACH * g + b].T, flip, preferred_element_type=jnp.float32).astype(jnp.bfloat16)
+            ts[:, EACH * g + b] = turned.reshape(NZ, depth, LANES)
+
+    def t_copy(g, j):
+        k = to(j)
+        return remote(
+            ts.at[k, pl.ds(EACH * g, EACH)], tall.at[z, pl.ds(EACH * g, EACH)], t_send.at[g, j], t_recv.at[g, j], zdev(k)
+        )
+
+    def start_targets(g):
+        def go(j, _):
+            t_copy(g, j).start()
+            return 0
+
+        lax.fori_loop(0, PEERS, go, 0)
+
+    for copy in t_loads[:EACH]:
+        copy.wait()
+    turn_targets(0)
+    pl.semaphore_wait(barrier, PEERS + 4 + jnp.where(last_x, 2, 0))
+
+    start_targets(0)
+
     position = lax.broadcasted_iota(jnp.int32, (8, LANES), 1)
     place = lax.broadcasted_iota(jnp.int32, (8, LANES), 0)
     lengths = jnp.zeros((8, LANES), jnp.int32)
@@ -100,31 +127,7 @@
             kept = jnp.where(at < qln[k], q_scale[k : k + 1, cols], 0.0)
             q_rows.append(jnp.where(q_mask[k : k + 1, cols] == 1, kept, 0.0))
     wown[...] = jnp.concatenate([t_weight] + q_rows, axis=0).astype(jnp.bfloat16)
-    hown[...] = jnp.zeros_like(hown)
-    hown[0:2, 0:8] = h_in[...]
-
-    def turn_targets(g):
-        for b in range(2):
-            turned = jnp.dot(tin[2 * g + b].T, flip, preferred_element_type=jnp.float32).astype(jnp.bfloat16)
-            ts[:, 2 * g + b] = turned.reshape(NZ, depth, LANES)
-
-    def t_copy(g, j):
-        k = to(j)
-        return remote(
-            ts.at[k, pl.ds(2 * g, 2)], tall.at[z, pl.ds(2 * g, 2)], t_send.at[g, j], t_recv.at[g, j], zdev(k)
-        )
-
-    def start_targets(g):
-        def go(j, _):
-            t_copy(g, j).start()
-            return 0
-
-        lax.fori_loop(0, PEERS, go, 0)
-
-    t_loads[0].wait()
-    t_loads[1].wait()
-    turn_targets(0)
-    pl.semaphore_wait(barrier, PEERS + 4 + jnp.where(last_x, 2, 0))
+    hown[...] = jnp.concatenate([h_in[0:1], h_in[1:2], jnp.zeros((1, LANES - 16), jnp.int32)], axis=1)
 
     shift_w = [remote(wown, wps.at[i], m_send.at[i], m_recv.at[i], shifted(i + 1)) for i in range(2)]
     for copy in shift_w:
@@ -150,8 +153,6 @@
     for copy in own_small:
         copy.start()
 
-    start_targets(0)
-
     s2 = [remote(q_hbm.at[k], qb.at[1, k], s2_send.at[k], s2_recv.at[k], shifted(2)) for k in range(2)]
     s1_even = [remote(q_hbm.at[k], qb.at[0, k], s1_send.at[k], s1_recv.at[k], core_dev) for k in range(2)]
     s1_odd = [remote(qb.at[1, k], qb.at[0, k], s1_send.at[k], s1_recv.at[k], core_dev) for k in range(2)]
@@ -172,7 +173,7 @@
         for copy in s1_even:
             copy.start()
 
-    for copy in t_loads[2:]:
+    for copy in t_loads[EACH:]:
         copy.wait()
 
     def send_targets(g, _):
@@ -184,7 +185,7 @@
 
         return 0
 
-    lax.fori_loop(1, 4, send_targets, 0)
+    lax.fori_loop(1, GROUPS, send_targets, 0)
     own_t = pltpu.make_async_copy(ts.at[z], tall.at[z], own_sem.at[3])
     own_t.start()
 
@@ -207,7 +208,7 @@
         turned = qin[c // 2, rows, :].T
         qs[:, c] = turned.reshape(NZ, depth, half)
 
-        @pl.when(c + 4 < AHEAD)
+        @pl.when(c + GROUPS < AHEAD)
         def _():
             start_chunk(c)
 
@@ -218,7 +219,7 @@
     own_q.start()
 
     def y_copy(g, i, src):
-        part = pl.ds(2 * g, 2)
+        part = pl.ds(EACH * g, EACH)
         return remote(tall.at[src, part], tall.at[NZ + src, part], y_send.at[g, i], y_recv.at[g, i], y_dev)
 
     own_t.wait()
@@ -231,13 +232,13 @@
             y_copy(g, j, frm(j)).start()
             later = g + AHEAD
 
-            @pl.when(later < 4)
+            @pl.when(later < GROUPS)
             def _():
                 t_copy(later, j).start()
 
-            @pl.when(jnp.logical_and(later >= 4, later < 8))
+            @pl.when(jnp.logical_and(later >= GROUPS, later < GROUPS + CHUNKS))
             def _():
-                q_copy(later - 4, j).start()
+                q_copy(later - GROUPS, j).start()
 
             return 0
 
@@ -250,7 +251,7 @@
 
         return 0
 
-    lax.fori_loop(0, 4, pass_on, 0)
+    lax.fori_loop(0, GROUPS, pass_on, 0)
 
     def wait_small(j, _):
         for copy in small(j):
@@ -382,7 +383,7 @@
         y_copy(g, PEERS, z).wait()
         return 0
 
-    lax.fori_loop(0, 4, wait_y, 0)
+    lax.fori_loop(0, GROUPS, wait_y, 0)
 
     def p_copy(part, j):
         k = to(j)
@@ -417,7 +418,7 @@
             for pair in range(4):
                 where = []
                 for u in range(2):
-                    hit = lax.rem(hs[zq, tile, 2 * pair + u], 2 * NZ * 8)
+                    hit = lax.rem(hs[zq, 0, tile * 8 + 2 * pair + u], 2 * NZ * 8)
                     owner, block = hit // 8, lax.rem(hit, 8)
                     other = jnp.where(lax.rem(owner, 2) == yh, 0, NZ)
                     where.append((other + owner // 2, block))
@@ -446,7 +447,7 @@
     prec[z] = psum[z]
 
     def sent(j, _):
-        for g in range(4):
+        for g in range(GROUPS):
             t_copy(g, j).wait_send()
         for c in range(CHUNKS):
             q_copy(c, j).wait_send()
@@ -504,9 +505,9 @@
             vmem((2 * NZ, 16, LANES), bf),
             vmem((2, 16, LANES), bf),
             vmem((2 * NZ, blocks, 8, cols), f32),
-            vmem((8, LANES), jnp.int32),
-            vmem((NZ, 8, LANES), jnp.int32),
-            pltpu.SMEM((NZ, 8, LANES), jnp.int32),
+            vmem((1, LANES), jnp.int32),
+            vmem((NZ, 1, LANES), jnp.int32),
+            pltpu.SMEM((NZ, 1, LANES), jnp.int32),
             vmem((NZ * tiles, rows, LANES), f32),
             vmem((2 * tiles, rows, LANES), f32),
             vmem((rows, 2 * LANES), f32),
@@ -516,9 +517,9 @@
             vmem((rows, width), bf),
             dma((10,)),
             dma((6,)),
-            dma((4, PEERS)), dma((4, PEERS)),
+            dma((GROUPS, PEERS)), dma((GROUPS, PEERS)),
             dma((CHUNKS, PEERS)), dma((CHUNKS, PEERS)),
-            dma((4, NZ)), dma((4, NZ)),
+            dma((GROUPS, NZ)), dma((GROUPS, NZ)),
             dma((2,)), dma((2,)),
             dma((2,)), dma((2,)),
             dma((2, PEERS)), dma((2, PEERS)),

time: 142 us -> 139 us (0.979)
  Pallas kernels: 138 us -> 136 us
    pallas_call x1, Pallas kernels: 138 us -> 136 us  [shards(): pl.pallas_call(kernel, out_shape=(jax.ShapeDtypeStruct((2, blocks, tiles,...]
where the time goes in v4:
time: 139 us
  Pallas kernels  136 us (98%)
  local copies, waits for them, and re-layouts  2.76 us (2%)
    pallas_call x1, Pallas kernels, shards(): pl.pallas_call(kernel, out_shape=(jax.ShapeDtypeStruct((2, blocks, tiles,...  136 us

profile of v4, /device:TPU:6, one launch (start us, length us, event | category | flops | bytes accessed | tf_op | source)
XLA Modules:
  0.0 139.1 jit_solution(15758361721501394183)
XLA Ops:
  0.6 135.7 %shard_map.104 = (f32[2,8,2,640]{3,2,1,0:T(2,128)}, f32[2,8]{1,0:T(2,128)}) custom-call(bf16[2,512,1280]{2,1,0:T(8,128)(2,1)} %q_hbm.1, bf16[2,512]{1,0:T(2,128)(2,1)} %qsc.1, s32[2,512]{1,0:T(2,128)} %qmk.1, s32[2]{0:T(128)} %qln.1, bf16[8,128,1280]{2,1,0:T(8,128)(2,1)} %t_hbm.1, bf16[8,128]{1,0:T(8,128)(2,1)} %tsc.1, s32[8,128]{1,0:T(8,128)} %tmk.1, ...), custom_call_target="tpu_custom_call" | custom-call | tf_op jit(solution)/shard_map/pallas_call | solution.py:488
  136.3 1.5 %copy.13 = f32[2,8,2,640]{3,2,1,0:T(2,128)} copy(f32[2,8,2,640]{3,2,1,0:T(2,128)} %get-tuple-element.4) | data formatting | bytes 163840
  137.8 1.2 copy.14

commit v5 on v4

--- a/solution.py
+++ b/solution.py
@@ -9,7 +9,7 @@
 LANES = 128
 NZ = 8
 PEERS = NZ - 1
-AHEAD = 4
+AHEAD = 5
 GROUPS = 2
 EACH = 8 // GROUPS
 CHUNKS = 4
@@ -59,7 +59,7 @@
 
     t_loads = [pltpu.make_async_copy(t_hbm.at[b], tin.at[b], in_sem.at[b]) for b in range(8)]
     q_loads = [pltpu.make_async_copy(q_hbm.at[k], qin.at[k], in_sem.at[8 + k]) for k in range(2)]
-    for copy in t_loads + q_loads:
+    for copy in t_loads[:EACH]:
         copy.start()
 
     barrier = pltpu.get_barrier_semaphore()
@@ -104,6 +104,8 @@
 
     for copy in t_loads[:EACH]:
         copy.wait()
+    for copy in t_loads[EACH:] + q_loads:
+        copy.start()
     turn_targets(0)
     pl.semaphore_wait(barrier, PEERS + 4 + jnp.where(last_x, 2, 0))
 
@@ -438,12 +440,20 @@
                     psum[zq, tile, 2 * part + 2, row : row + 1, :] += row_sum(carry)
             return 0
 
-        lax.fori_loop(0, NZ, query, 0)
+        def peer(j, _):
+            query(to(j), 0)
+
+            @pl.when(jnp.logical_and(c == CHUNKS - 1, j < PEERS))
+            def _():
+                p_copy(2, j).start()
+
+            return 0
+
+        lax.fori_loop(0, NZ, peer, 0)
         return 0
 
     lax.fori_loop(0, CHUNKS, chunk, 0)
 
-    start_p(2)
     prec[z] = psum[z]
 
     def sent(j, _):

time: 139 us -> 139 us (level)
  no operation moved by 1% of the time
where the time goes in v5:
time: 139 us
  Pallas kernels  135 us (97%)
  local copies, waits for them, and re-layouts  2.76 us (2%)
    pallas_call x1, Pallas kernels, shards(): pl.pallas_call(kernel, out_shape=(jax.ShapeDtypeStruct((2, blocks, tiles,...  135 us

profile of v5, /device:TPU:6, one launch (start us, length us, event | category | flops | bytes accessed | tf_op | source)
XLA Modules:
  0.0 138.7 jit_solution(17647286895298317294)
XLA Ops:
  0.6 135.3 %shard_map.104 = (f32[2,8,2,640]{3,2,1,0:T(2,128)}, f32[2,8]{1,0:T(2,128)}) custom-call(bf16[2,512,1280]{2,1,0:T(8,128)(2,1)} %q_hbm.1, bf16[2,512]{1,0:T(2,128)(2,1)} %qsc.1, s32[2,512]{1,0:T(2,128)} %qmk.1, s32[2]{0:T(128)} %qln.1, bf16[8,128,1280]{2,1,0:T(8,128)(2,1)} %t_hbm.1, bf16[8,128]{1,0:T(8,128)(2,1)} %tsc.1, s32[8,128]{1,0:T(8,128)} %tmk.1, ...), custom_call_target="tpu_custom_call" | custom-call | tf_op jit(solution)/shard_map/pallas_call | solution.py:498
  135.9 1.5 %copy.13 = f32[2,8,2,640]{3,2,1,0:T(2,128)} copy(f32[2,8,2,640]{3,2,1,0:T(2,128)} %get-tuple-element.4) | data formatting | bytes 163840
  137.5 1.2 copy.14

commit v6 on v4

--- a/solution.py
+++ b/solution.py
@@ -59,7 +59,7 @@
 
     t_loads = [pltpu.make_async_copy(t_hbm.at[b], tin.at[b], in_sem.at[b]) for b in range(8)]
     q_loads = [pltpu.make_async_copy(q_hbm.at[k], qin.at[k], in_sem.at[8 + k]) for k in range(2)]
-    for copy in t_loads + q_loads:
+    for copy in t_loads[:EACH]:
         copy.start()
 
     barrier = pltpu.get_barrier_semaphore()
@@ -104,6 +104,8 @@
 
     for copy in t_loads[:EACH]:
         copy.wait()
+    for copy in t_loads[EACH:] + q_loads:
+        copy.start()
     turn_targets(0)
     pl.semaphore_wait(barrier, PEERS + 4 + jnp.where(last_x, 2, 0))
 

time: 139 us -> 139 us (level)
  no operation moved by 1% of the time
where the time goes in v6:
time: 139 us
  Pallas kernels  136 us (98%)
  local copies, waits for them, and re-layouts  2.76 us (2%)
    pallas_call x1, Pallas kernels, shards(): pl.pallas_call(kernel, out_shape=(jax.ShapeDtypeStruct((2, blocks, tiles,...  136 us

profile of v6, /device:TPU:6, one launch (start us, length us, event | category | flops | bytes accessed | tf_op | source)
XLA Modules:
  0.0 139.1 jit_solution(3283465518558559707)
XLA Ops:
  0.6 135.7 %shard_map.104 = (f32[2,8,2,640]{3,2,1,0:T(2,128)}, f32[2,8]{1,0:T(2,128)}) custom-call(bf16[2,512,1280]{2,1,0:T(8,128)(2,1)} %q_hbm.1, bf16[2,512]{1,0:T(2,128)(2,1)} %qsc.1, s32[2,512]{1,0:T(2,128)} %qmk.1, s32[2]{0:T(128)} %qln.1, bf16[8,128,1280]{2,1,0:T(8,128)(2,1)} %t_hbm.1, bf16[8,128]{1,0:T(8,128)(2,1)} %tsc.1, s32[8,128]{1,0:T(8,128)} %tmk.1, ...), custom_call_target="tpu_custom_call" | custom-call | tf_op jit(solution)/shard_map/pallas_call | solution.py:490
  136.3 1.5 %copy.13 = f32[2,8,2,640]{3,2,1,0:T(2,128)} copy(f32[2,8,2,640]{3,2,1,0:T(2,128)} %get-tuple-element.4) | data formatting | bytes 163840
  137.8 1.2 copy.14
